TPU v7x, 32 devices: a whole 2x2x4 slice. The times are simulated.
32 devices in a mesh: groups: 2 (over y), dp: 4 (over z), tensor: 4 (over x, core).
Axes of the slice: x: 2, y: 2, z: 4, core: 2. Of those that a mesh axis runs over, the one named last changes fastest.
Arguments:
- hidden_acts: bfloat16 [1024, 28672], P(('groups', 'dp'), 'tensor'), parts along dimension 0, may hold values from -40 to 40
- out_grads: bfloat16 [1024, 8192], P(('groups', 'dp'), 'tensor'), parts along dimension 0, may hold values from -40 to 40
- proj_in: bfloat16 [28672, 64], P('tensor'), may hold values from -0.03125 to 0.03125
- proj_out: bfloat16 [8192, 64], P('tensor'), may hold values from -0.0625 to 0.0625
- query_sketches: bfloat16 [64, 4096], P('dp'), may hold values from -0.09375 to 0.09375
Outputs:
- scores: float32 [2, 64], P('groups', 'dp'), parts along dimension 0
There are 2 independent parts, one for each index of `groups`. A program takes and returns all parts, laid end to end along the dimension named above; an argument that names none is the same for every part. Nothing has to cross between parts.
All inputs are finite; a program needn't handle non-finite values.
Results may differ from a plain program's by a relative error of at most 0.0032.
Values sent between devices are 32-bit elements; how exact they have to be, the bound alone decides.
A program may use at most 64 MiB of HBM per device.

v0:
```python
import math

import jax
import jax.numpy as jnp
from jax import lax
from jax.sharding import PartitionSpec as P


def inverse_of(cov):
    size = cov.shape[0]
    eye = jnp.eye(size, dtype=jnp.float32)
    damped = cov + 0.1 * jnp.trace(cov) / size * eye
    factor = jnp.linalg.cholesky(damped)
    return jax.scipy.linalg.cho_solve((factor, True), eye)


def shards(hidden_acts, out_grads, proj_in, proj_out, query_sketches):
    highest = lax.Precision.HIGHEST
    in_part = jnp.dot(hidden_acts, proj_in, preferred_element_type=jnp.float32)
    out_part = jnp.dot(out_grads, proj_out, preferred_element_type=jnp.float32)
    in_side, out_side = lax.psum((in_part, out_part), "tensor")
    local_in = jnp.dot(in_side.T, in_side, precision=highest)
    local_out = jnp.dot(out_side.T, out_side, precision=highest)
    partial_value = jnp.dot(in_side.T, out_side, precision=highest)
    rows = in_side.shape[0]
    width = in_side.shape[1]
    dp_size = lax.axis_size("dp")
    span = min(32, dp_size)
    seq_count = dp_size // span
    seq_index = lax.axis_index("dp") // span
    slot = (
        (jnp.arange(seq_count, dtype=jnp.int32) == seq_index)
        .astype(jnp.float32)
        .reshape(seq_count, 1, 1)
    )
    token_count = rows * dp_size
    factor = 1.0 / math.sqrt(rows * span)
    in_cov, out_cov = lax.psum((local_in, local_out), "dp")
    in_inv = inverse_of(in_cov / token_count)
    out_inv = inverse_of(out_cov / token_count)
    own_term = jnp.dot(
        jnp.dot(in_inv, partial_value, precision=highest), out_inv, precision=highest
    )
    precond = lax.psum(slot * own_term[None], "dp") * factor
    precond = precond.reshape(seq_count, width * width).astype(jnp.bfloat16)
    return jnp.dot(precond, query_sketches.T, preferred_element_type=jnp.float32)


def solution(mesh):
    return jax.shard_map(
        shards,
        mesh=mesh,
        in_specs=(
            P(("groups", "dp"), "tensor"),
            P(("groups", "dp"), "tensor"),
            P("tensor", None),
            P("tensor", None),
            P("dp", None),
        ),
        out_specs=P("groups", "dp"),
        check_vma=False,
    )
```

profile of v0, /device:TPU:0, one launch (start us, length us, event | category | flops | bytes accessed | tf_op | source)
XLA Modules:
  0.0 119.8 jit_solution(18115361708817011136)
XLA Ops:
  6.5 0.0 copy-start
  6.5 0.0 copy-start.2
  6.5 0.0 copy-start.1
  6.5 0.0 all-reduce.4.cloned.1.call-start
  6.5 1.5 %copy-done = bf16[128,7168]{1,0:T(8,128)(2,1)S(1)} copy-done((bf16[128,7168]{1,0:T(8,128)(2,1)S(1)}, bf16[128,7168]{1,0:T(8,128)(2,1)}, u32[]{:S(2)}) %copy-start) | copy-done | bytes 1835032
  8.0 2.5 %fusion.15 = f32[128,64]{0,1:T(8,128)} fusion(bf16[128,7168]{1,0:T(8,128)(2,1)S(1)} %copy-done, bf16[7168,64]{0,1:T(8,128)(2,1)} %param.10), kind=kOutput, calls=%fused_computation.32 | convolution fusion | flops 117440512 | bytes 2785280 | tf_op jit(solution)/shard_map/dot_general | solution.py:19
  10.6 0.0 copy-done.2
  10.6 0.0 copy-done.1
  10.6 0.0 copy-start.3
  10.6 0.9 fusion.17
  11.5 0.0 all-reduce.4.cloned.1.call-update
  11.5 34.0 %all-reduce.4.cloned.1.call-done = (f32[128,64]{0,1:T(8,128)}, f32[128,64]{0,1:T(8,128)}) async-done(((f32[128,64]{0,1:T(8,128)}, f32[128,64]{0,1:T(8,128)}), (f32[128,64]{0,1:T(8,128)}, f32[128,64]{0,1:T(8,128)})) %all-reduce.4.cloned.1.call-update) | async-done | bytes 65552 | tf_op jit(solution)/shard_map/psum | solution.py:21
  45.5 1.0 fusion.20
  46.5 1.0 fusion.18
  47.5 1.0 fusion.16
  48.5 19.6 %all-reduce.1 = (f32[64,64]{0,1:T(8,128)S(1)}, f32[64,64]{0,1:T(8,128)S(1)}) all-reduce(f32[64,64]{0,1:T(8,128)S(1)} %fusion.16, f32[64,64]{0,1:T(8,128)S(1)} %fusion.20), channel_id=1, replica_groups=mesh['groups'=2,'dp'=4,'tensor'=4] {'dp'}, use_global_device_ids=true, to_apply=%region_1.0 | all-reduce | flops 8192 | bytes 65536 | tf_op jit(solution)/shard_map/psum | solution.py:38
  68.2 0.6 select_reduce_fusion.2
  68.8 0.7 select_reduce_fusion.3
  70.8 0.1 copy.9
  70.9 5.8 %cholesky.55 = f32[64,64]{1,0:T(8,128)S(1)} custom-call(f32[64,64]{1,0:T(8,128)S(1)} %fusion.10), custom_call_target="Cholesky" | custom-call | tf_op jit(solution)/shard_map/jit(cholesky)/cholesky | solution.py:13
  76.8 0.6 compare_reduce_fusion
  77.5 0.7 fusion.6
  78.1 4.9 %custom-call.9 = f32[1,64,64]{1,2,0:T(8,128)S(1)} custom-call(f32[1,64,64]{2,1,0:T(8,128)S(1)} %fusion.6), custom_call_target="InvertDiagBlocksLowerTriangular" | custom-call | tf_op jit(solution)/shard_map/jit(_cho_solve)/triangular_solve | solution.py:14
  83.0 0.3 fusion.1
  83.3 0.2 fusion.7
  83.4 0.1 copy.7
  83.5 5.8 %cholesky.44 = f32[64,64]{1,0:T(8,128)S(1)} custom-call(f32[64,64]{1,0:T(8,128)S(1)} %fusion.14), custom_call_target="Cholesky" | custom-call | tf_op jit(solution)/shard_map/jit(cholesky)/cholesky | solution.py:13
  89.4 0.6 compare_reduce_fusion.1
  90.1 0.7 fusion.5
  90.7 4.9 %custom-call.8 = f32[1,64,64]{1,2,0:T(8,128)S(1)} custom-call(f32[1,64,64]{2,1,0:T(8,128)S(1)} %fusion.5), custom_call_target="InvertDiagBlocksLowerTriangular" | custom-call | tf_op jit(solution)/shard_map/jit(_cho_solve)/triangular_solve | solution.py:14
  95.6 0.3 fusion.3
  95.9 0.2 fusion.11
  96.0 0.2 fusion.19
  96.2 0.2 fusion
  96.4 15.8 %psum.39 = f32[1,64,64]{2,1,0:T(8,128)S(1)} all-reduce(f32[1,64,64]{2,1,0:T(8,128)S(1)} %fusion), channel_id=1, replica_groups=mesh['groups'=2,'dp'=4,'tensor'=4] {'dp'}, use_global_device_ids=true, to_apply=%region_8.11 | all-reduce | flops 4096 | bytes 32768 | tf_op jit(solution)/shard_map/psum | solution.py:44
  112.2 0.1 reshape.27
  112.3 0.0 copy-done.3
  112.3 0.7 fusion.21
  (6 shorter events, 0.1 us)
Async XLA Ops:
  6.5 1.5 %copy-start = (bf16[128,7168]{1,0:T(8,128)(2,1)S(1)}, bf16[128,7168]{1,0:T(8,128)(2,1)}, u32[]{:S(2)}) copy-start(bf16[128,7168]{1,0:T(8,128)(2,1)} %param.8) | copy-start | bytes 5505028
  6.5 4.0 %copy-start.2 = (bf16[2048,64]{0,1:T(8,128)(2,1)S(1)}, bf16[2048,64]{0,1:T(8,128)(2,1)}, u32[]{:S(2)}) copy-start(bf16[2048,64]{0,1:T(8,128)(2,1)} %param.11) | copy-start | bytes 786436
  6.5 4.0 %copy-start.1 = (bf16[128,2048]{1,0:T(8,128)(2,1)S(1)}, bf16[128,2048]{1,0:T(8,128)(2,1)}, u32[]{:S(2)}) copy-start(bf16[128,2048]{1,0:T(8,128)(2,1)} %param.9) | copy-start | bytes 1572868
  6.5 39.0 %all-reduce.4.cloned.1.call-start = ((), (), s32[]{:S(2)}) async-start(), calls=%async_computation | async-start | bytes 131072 | tf_op jit(solution)/shard_map/psum | solution.py:21
  10.6 101.7 %copy-start.3 = (bf16[16,4096]{1,0:T(8,128)(2,1)S(1)}, bf16[16,4096]{1,0:T(8,128)(2,1)}, u32[]{:S(2)}) copy-start(bf16[16,4096]{1,0:T(8,128)(2,1)} %param.12) | copy-start | bytes 393220
Sparse Core Ops, SparseCore 0:
  11.6 33.8 all-reduce.3
where the time goes:
time: 120 us
  blocking collectives  35.4 us (30%)
  waiting for transfers between devices  34 us (28%)
  other arithmetic  25.5 us (21%)
  between operations  14.9 us (12%)
  matrix products  8.24 us (7%)
  local copies, waits for them, and re-layouts  1.74 us (1%)
    psum x1, waiting for transfers between devices, shards(): in_side, out_side = lax.psum((in_part, out_part), 'tensor')  34 us
    psum x1, blocking collectives, shards(): in_cov, out_cov = lax.psum((local_in, local_out), 'dp')  19.6 us
    psum x1, blocking collectives, shards(): precond = lax.psum(slot * own_term[None], 'dp') * factor  15.8 us
    another operation x6, other arithmetic, inverse_of(): factor = jnp.linalg.cholesky(damped)  13 us
    another operation x4, other arithmetic, inverse_of(): return jax.scipy.linalg.cho_solve((factor, True), eye)  11.1 us
    dot_general x1, matrix products, shards(): in_part = jnp.dot(hidden_acts, proj_in, preferred_element_type=jnp.float32)  2.53 us
  transfers between devices with their start and end apart: 1, of which 1 were waited for; matrix products, arithmetic and copies ran while one was open for 0% of the time, Pallas kernels for 0%

commit v1 on v0

v1 whole, which is shorter than its diff:
```python
import functools
import math

import jax
import jax.numpy as jnp
from jax import lax
from jax.experimental import pallas as pl
from jax.experimental.pallas import tpu as pltpu
from jax.sharding import PartitionSpec as P

MESH = pl.DeviceIdType.MESH
HIGHEST = lax.Precision.HIGHEST
IN_CHUNKS = 4
BLOCK = 4


def repeat(start, stop, body):
    if stop - start <= 8:
        for k in range(start, stop):
            body(k)
    else:
        lax.fori_loop(start, stop, lambda k, c: (body(k), c)[1], 0)


def negated_inverses(both, width):
    shape = both.shape
    row = lax.broadcasted_iota(jnp.int32, shape, 0)
    lane = lax.broadcasted_iota(jnp.int32, shape, 1)
    col = lane % width
    side = lane - col
    lane1 = lax.broadcasted_iota(jnp.int32, (1, shape[1]), 1)
    col1 = lane1 % width
    m = both
    for k0 in range(0, width, BLOCK):
        js = range(BLOCK)
        cols = [jnp.take_along_axis(m, side + (k0 + j), axis=1) for j in js]
        d = [[cols[j][k0 + i : k0 + i + 1, :] for j in js] for i in js]
        in_block1 = (col1 >= k0) & (col1 < k0 + BLOCK)
        w = [
            jnp.where(in_block1, jnp.where(col1 == k0 + i, -1.0, 0.0), m[k0 + i : k0 + i + 1, :])
            for i in js
        ]
        for p in js:
            r = 1.0 / d[p][p]
            w[p] = w[p] * r
            for j in range(p + 1, BLOCK):
                d[p][j] = d[p][j] * r
            for i in js:
                if i != p:
                    f = d[i][p]
                    w[i] = w[i] - f * w[p]
                    for j in range(p + 1, BLOCK):
                        d[i][j] = d[i][j] - f * d[p][j]
        in_rows = (row >= k0) & (row < k0 + BLOCK)
        in_cols = (col >= k0) & (col < k0 + BLOCK)
        m = jnp.where(in_rows | in_cols, 0.0, m)
        for j in js:
            c = jnp.where(in_rows, jnp.where(row == k0 + j, -1.0, 0.0), cols[j])
            m = m - c * w[j]
    return m


def kernel(
    n_t, n_dp, h_hbm, g_hbm, pi_hbm, po_hbm, q_hbm, out_ref,
    h_v, g_v, pi_v, po_v, q_v, part, landed, tokens, pay,
    load_sem, h_sem, a_send, a_recv, b_send, b_recv, c_send, c_recv,
):
    me_t = lax.axis_index("tensor")
    me_dp = lax.axis_index("dp")
    width = pi_v.shape[0]
    rows = part.shape[0]
    share = rows // n_t
    span = min(32, n_dp)
    seqs = n_dp // span
    token_count = rows * n_dp
    factor = 1.0 / math.sqrt(rows * span)

    step = h_v.shape[1] // IN_CHUNKS
    loads = [
        pltpu.make_async_copy(g_hbm, g_v, load_sem.at[0]),
        pltpu.make_async_copy(po_hbm, po_v, load_sem.at[1]),
    ]
    chunks = []
    for c in range(IN_CHUNKS):
        at = pl.ds(c * step, step)
        chunks.append(
            (
                pltpu.make_async_copy(h_hbm.at[:, at], h_v.at[:, at], h_sem.at[2 * c]),
                pltpu.make_async_copy(pi_hbm.at[:, at], pi_v.at[:, at], h_sem.at[2 * c + 1]),
            )
        )
    q_load = pltpu.make_async_copy(q_hbm, q_v, load_sem.at[2])
    for copy in loads:
        copy.start()
    for pair in chunks:
        for copy in pair:
            copy.start()
    q_load.start()

    barrier = pltpu.get_barrier_semaphore()

    def greet_t(k):
        pl.semaphore_signal(barrier, inc=1, device_id={"tensor": lax.rem(me_t + k, n_t)}, device_id_type=MESH)

    def greet_dp(k):
        pl.semaphore_signal(barrier, inc=1, device_id={"dp": lax.rem(me_dp + k, n_dp)}, device_id_type=MESH)

    repeat(1, n_t, greet_t)
    repeat(1, n_dp, greet_dp)

    nt = (((1,), (1,)), ((), ()))
    tn = (((0,), (0,)), ((), ()))
    for copy in loads:
        copy.wait()
    part[:, width:] = lax.dot_general(g_v[...], po_v[...], nt, preferred_element_type=jnp.float32)
    total = None
    for c, pair in enumerate(chunks):
        for copy in pair:
            copy.wait()
        at = pl.ds(c * step, step)
        term = lax.dot_general(h_v[:, at], pi_v[:, at], nt, preferred_element_type=jnp.float32)
        total = term if total is None else total + term
    part[:, :width] = total

    pl.semaphore_wait(barrier, (n_t - 1) + (n_dp - 1))

    def a_copy(k):
        peer = lax.rem(me_t + k, n_t)
        return pltpu.make_async_remote_copy(
            src_ref=part.at[pl.ds(pl.multiple_of(peer * share, share), share)],
            dst_ref=landed.at[k - 1],
            send_sem=a_send.at[k - 1],
            recv_sem=a_recv.at[k - 1],
            device_id={"tensor": peer},
            device_id_type=MESH,
        )

    a_copies = [a_copy(k) for k in range(1, n_t)]
    for copy in a_copies:
        copy.start()
    mine = part[pl.ds(pl.multiple_of(me_t * share, share), share), :]
    for k, copy in enumerate(a_copies):
        copy.wait_recv()
        mine = mine + landed[k]
    tokens[me_dp] = mine

    def b_copy(k, slot):
        return pltpu.make_async_remote_copy(
            src_ref=tokens.at[slot],
            dst_ref=tokens.at[slot],
            send_sem=b_send.at[k - 1],
            recv_sem=b_recv.at[k - 1],
            device_id={"dp": lax.rem(me_dp + k, n_dp)},
            device_id_type=MESH,
        )

    repeat(1, n_dp, lambda k: b_copy(k, me_dp).start())
    repeat(1, n_dp, lambda k: b_copy(k, lax.rem(me_dp + n_dp - k, n_dp)).wait_recv())

    upper = lax.broadcasted_iota(jnp.int32, (width, 2 * width), 1) >= width
    upper_half = lax.broadcasted_iota(jnp.int32, (width // 2, 2 * width), 1) >= width
    upper1 = lax.broadcasted_iota(jnp.int32, (1, 2 * width), 1) >= width
    half = width // 2
    covs = None
    for s in range(seqs):
        own = tokens[s * span : (s + 1) * span].reshape(span * share, 2 * width)
        gram = lax.dot_general(own, own, tn, precision=HIGHEST, preferred_element_type=jnp.float32)
        cov = jnp.where(upper, gram[width:], gram[:width])
        covs = cov if covs is None else covs + cov
        swapped = pltpu.roll(gram[half:width], width, 1)
        pay[me_t, pl.ds(width + s * half, half), :] = jnp.where(upper_half, gram[:half], swapped)
    pay[me_t, :width, :] = covs

    def c_copy(k, slot):
        return pltpu.make_async_remote_copy(
            src_ref=pay.at[slot],
            dst_ref=pay.at[slot],
            send_sem=c_send.at[k - 1],
            recv_sem=c_recv.at[k - 1],
            device_id={"tensor": lax.rem(me_t + k, n_t)},
            device_id_type=MESH,
        )

    for k in range(1, n_t):
        c_copy(k, me_t).start()
    for k in range(1, n_t):
        c_copy(k, lax.rem(me_t + n_t - k, n_t)).wait_recv()
    full = pay[0]
    for t in range(1, n_t):
        full = full + pay[t]

    both = full[:width] / token_count
    row = lax.broadcasted_iota(jnp.int32, both.shape, 0)
    col = lax.broadcasted_iota(jnp.int32, both.shape, 1) % width
    diag = jnp.sum(jnp.where(row == col, both, 0.0), axis=0, keepdims=True)
    trace_in = jnp.sum(jnp.where(upper1, 0.0, diag), axis=1, keepdims=True)
    trace_out = jnp.sum(jnp.where(upper1, diag, 0.0), axis=1, keepdims=True)
    damp = 0.1 * jnp.where(upper1, trace_out, trace_in) / width
    both = both + jnp.where(row == col, damp, 0.0)
    inverse = negated_inverses(both, width)
    in_inv = inverse[:, :width]
    out_inv = jnp.where(upper, inverse, pltpu.roll(inverse, width, 1))

    q_load.wait()
    for s in range(seqs):
        packed = full[width + s * half : width + (s + 1) * half]
        sketch = jnp.concatenate([pltpu.roll(packed, width, 1)[:, :width], packed[:, :width]], axis=0)
        left = jnp.dot(in_inv, sketch, precision=HIGHEST, preferred_element_type=jnp.float32)
        precond = jnp.dot(left, out_inv, precision=HIGHEST, preferred_element_type=jnp.float32)
        precond = (precond * factor).astype(jnp.bfloat16).astype(jnp.float32)
        sums = [None] * 4
        for j in range(half):
            weights = jnp.where(upper1, precond[2 * j + 1 : 2 * j + 2, :], precond[2 * j : 2 * j + 1, :])
            term = q_v[:, 2 * width * j : 2 * width * (j + 1)].astype(jnp.float32) * weights
            sums[j % 4] = term if sums[j % 4] is None else sums[j % 4] + term
        acc = (sums[0] + sums[1]) + (sums[2] + sums[3])
        ones = jnp.ones((8, 2 * width), jnp.float32)
        scores = lax.dot_general(ones, acc, nt, precision=HIGHEST, preferred_element_type=jnp.float32)
        out_ref[s : s + 1, :] = scores[:1]

    for copy in a_copies:
        copy.wait_send()
    repeat(1, n_dp, lambda k: b_copy(k, me_dp).wait_send())
    for k in range(1, n_t):
        c_copy(k, me_t).wait_send()


def solution(mesh):
    n_t, n_dp = mesh.shape["tensor"], mesh.shape["dp"]

    def shards(hidden_acts, out_grads, proj_in, proj_out, query_sketches):
        rows, depth = hidden_acts.shape
        model = out_grads.shape[1]
        width = proj_in.shape[1]
        queries, flat = query_sketches.shape
        seqs = n_dp // min(32, n_dp)
        share = rows // n_t
        dma = pltpu.SemaphoreType.DMA
        f32, bf16 = jnp.float32, jnp.bfloat16
        return pl.pallas_call(
            functools.partial(kernel, n_t, n_dp),
            out_shape=jax.ShapeDtypeStruct((seqs, queries), f32),
            in_specs=[pl.BlockSpec(memory_space=pl.ANY)] * 5,
            out_specs=pl.BlockSpec(memory_space=pltpu.VMEM),
            scratch_shapes=[
                pltpu.VMEM((rows, depth), bf16),
                pltpu.VMEM((rows, model), bf16),
                pltpu.VMEM((width, depth), bf16),
                pltpu.VMEM((width, model), bf16),
                pltpu.VMEM((queries, flat), bf16),
                pltpu.VMEM((rows, 2 * width), f32),
                pltpu.VMEM((n_t - 1, share, 2 * width), f32),
                pltpu.VMEM((n_dp, share, 2 * width), f32),
                pltpu.VMEM((n_t, width + seqs * (width // 2), 2 * width), f32),
                dma((3,)),
                dma((2 * IN_CHUNKS,)),
                dma((n_t - 1,)),
                dma((n_t - 1,)),
                dma((n_dp - 1,)),
                dma((n_dp - 1,)),
                dma((n_t - 1,)),
                dma((n_t - 1,)),
            ],
            compiler_params=pltpu.CompilerParams(
                collective_id=0, has_side_effects=True, vmem_limit_bytes=48 * 1024 * 1024
            ),
        )(hidden_acts, out_grads, proj_in.T, proj_out.T, query_sketches)

    return jax.shard_map(
        shards,
        mesh=mesh,
        in_specs=(
            P(("groups", "dp"), "tensor"),
            P(("groups", "dp"), "tensor"),
            P("tensor", None),
            P("tensor", None),
            P("dp", None),
        ),
        out_specs=P("groups", "dp"),
        check_vma=False,
    )
```

time: 120 us -> 25.3 us (0.21)
  the two profiles are of different devices: /device:TPU:0 before, /device:TPU:1 now
where the time goes in v1:
time: 25.3 us; the launch traced here: 24.9 us
  Pallas kernels  18.8 us (74%)
  local copies, waits for them, and re-layouts  6.08 us (24%)
    pallas_call x1, Pallas kernels, shards(): pl.pallas_call(functools.partial(kernel, n_t, n_dp), out_shape=jax.ShapeD...  18.8 us
    unnamed x11, local copies, waits for them, and re-layouts  6.08 us

profile of v1, /device:TPU:1, one launch (start us, length us, event | category | flops | bytes accessed | tf_op | source)
XLA Modules:
  0.0 24.9 jit_solution(10420164195650882115)
XLA Ops:
  0.0 0.0 copy-start
  0.0 1.5 %copy-done = bf16[128,7168]{1,0:T(8,128)(2,1)S(1)} copy-done((bf16[128,7168]{1,0:T(8,128)(2,1)S(1)}, bf16[128,7168]{1,0:T(8,128)(2,1)}, u32[]{:S(2)}) %copy-start) | copy-done | bytes 1835032
  1.5 0.0 copy-start.1
  1.5 1.2 %copy-done.1 = bf16[7168,64]{0,1:T(8,128)(2,1)S(1)} copy-done((bf16[7168,64]{0,1:T(8,128)(2,1)S(1)}, bf16[7168,64]{0,1:T(8,128)(2,1)}, u32[]{:S(2)}) %copy-start.1) | copy-done | bytes 917528
  2.7 0.0 copy-start.2
  2.7 1.0 %copy-done.2 = bf16[128,2048]{1,0:T(8,128)(2,1)S(1)} copy-done((bf16[128,2048]{1,0:T(8,128)(2,1)S(1)}, bf16[128,2048]{1,0:T(8,128)(2,1)}, u32[]{:S(2)}) %copy-start.2) | copy-done | bytes 524312
  3.7 0.0 copy-start.3
  3.7 0.9 %copy-done.3 = bf16[2048,64]{0,1:T(8,128)(2,1)S(1)} copy-done((bf16[2048,64]{0,1:T(8,128)(2,1)S(1)}, bf16[2048,64]{0,1:T(8,128)(2,1)}, u32[]{:S(2)}) %copy-start.3) | copy-done | bytes 262168
  4.7 0.0 copy-start.4
  4.7 0.9 %copy-done.4 = bf16[16,4096]{1,0:T(8,128)(2,1)S(1)} copy-done((bf16[16,4096]{1,0:T(8,128)(2,1)S(1)}, bf16[16,4096]{1,0:T(8,128)(2,1)}, u32[]{:S(2)}) %copy-start.4) | copy-done | bytes 131096
  5.6 18.8 %shard_map.55 = f32[1,16]{1,0:T(1,128)S(1)} custom-call(bf16[128,7168]{1,0:T(8,128)(2,1)S(1)} %copy-done, bf16[128,2048]{1,0:T(8,128)(2,1)S(1)} %copy-done.2, bf16[64,7168]{1,0:T(8,128)(2,1)S(1)} %bitcast.2, bf16[64,2048]{1,0:T(8,128)(2,1)S(1)} %bitcast.3, bf16[16,4096]{1,0:T(8,128)(2,1)S(1)} %copy-done.4), custom_call_target="tpu_custom_call" | custom-call | tf_op jit(solution)/shard_map/pallas_call | solution.py:240
  24.4 0.5 %copy.7 = f32[1,16]{1,0:T(1,128)} copy(f32[1,16]{1,0:T(1,128)S(1)} %shard_map.55) | data formatting | bytes 128
Async XLA Ops:
  0.0 1.5 %copy-start = (bf16[128,7168]{1,0:T(8,128)(2,1)S(1)}, bf16[128,7168]{1,0:T(8,128)(2,1)}, u32[]{:S(2)}) copy-start(bf16[128,7168]{1,0:T(8,128)(2,1)} %h_hbm.1) | copy-start | bytes 5505028
  1.5 1.2 %copy-start.1 = (bf16[7168,64]{0,1:T(8,128)(2,1)S(1)}, bf16[7168,64]{0,1:T(8,128)(2,1)}, u32[]{:S(2)}) copy-start(bf16[7168,64]{0,1:T(8,128)(2,1)} %param.7) | copy-start | bytes 2752516
  2.7 1.0 %copy-start.2 = (bf16[128,2048]{1,0:T(8,128)(2,1)S(1)}, bf16[128,2048]{1,0:T(8,128)(2,1)}, u32[]{:S(2)}) copy-start(bf16[128,2048]{1,0:T(8,128)(2,1)} %g_hbm.1) | copy-start | bytes 1572868
  3.7 0.9 %copy-start.3 = (bf16[2048,64]{0,1:T(8,128)(2,1)S(1)}, bf16[2048,64]{0,1:T(8,128)(2,1)}, u32[]{:S(2)}) copy-start(bf16[2048,64]{0,1:T(8,128)(2,1)} %param.8) | copy-start | bytes 786436
  4.7 0.9 %copy-start.4 = (bf16[16,4096]{1,0:T(8,128)(2,1)S(1)}, bf16[16,4096]{1,0:T(8,128)(2,1)}, u32[]{:S(2)}) copy-start(bf16[16,4096]{1,0:T(8,128)(2,1)} %q_hbm.1) | copy-start | bytes 393220

commit v2 on v1

--- a/solution.py
+++ b/solution.py
@@ -11,7 +11,7 @@
 MESH = pl.DeviceIdType.MESH
 HIGHEST = lax.Precision.HIGHEST
 IN_CHUNKS = 4
-BLOCK = 4
+BLOCK = 8
 
 
 def repeat(start, stop, body):
@@ -20,6 +20,10 @@
             body(k)
     else:
         lax.fori_loop(start, stop, lambda k, c: (body(k), c)[1], 0)
+
+
+def pair_of(n_t):
+    return 2 if n_t % 2 == 0 else 1
 
 
 def negated_inverses(both, width):
@@ -62,11 +66,14 @@
 
 def kernel(
     n_t, n_dp, h_hbm, g_hbm, pi_hbm, po_hbm, q_hbm, out_ref,
-    h_v, g_v, pi_v, po_v, q_v, part, landed, tokens, pay,
+    h_v, g_v, pi_v, po_v, q_v, part, landed, tokens,
     load_sem, h_sem, a_send, a_recv, b_send, b_recv, c_send, c_recv,
 ):
     me_t = lax.axis_index("tensor")
     me_dp = lax.axis_index("dp")
+    pair = pair_of(n_t)
+    groups = n_t // pair
+    other = me_t + 1 - 2 * lax.rem(me_t, 2)
     width = pi_v.shape[0]
     rows = part.shape[0]
     share = rows // n_t
@@ -92,8 +99,8 @@
     q_load = pltpu.make_async_copy(q_hbm, q_v, load_sem.at[2])
     for copy in loads:
         copy.start()
-    for pair in chunks:
-        for copy in pair:
+    for copies in chunks:
+        for copy in copies:
             copy.start()
     q_load.start()
 
@@ -103,7 +110,9 @@
         pl.semaphore_signal(barrier, inc=1, device_id={"tensor": lax.rem(me_t + k, n_t)}, device_id_type=MESH)
 
     def greet_dp(k):
-        pl.semaphore_signal(barrier, inc=1, device_id={"dp": lax.rem(me_dp + k, n_dp)}, device_id_type=MESH)
+        for m in range(groups):
+            peer = {"dp": lax.rem(me_dp + k, n_dp), "tensor": lax.rem(me_t + m * pair, n_t)}
+            pl.semaphore_signal(barrier, inc=1, device_id=peer, device_id_type=MESH)
 
     repeat(1, n_t, greet_t)
     repeat(1, n_dp, greet_dp)
@@ -114,15 +123,15 @@
         copy.wait()
     part[:, width:] = lax.dot_general(g_v[...], po_v[...], nt, preferred_element_type=jnp.float32)
     total = None
-    for c, pair in enumerate(chunks):
-        for copy in pair:
+    for c, copies in enumerate(chunks):
+        for copy in copies:
             copy.wait()
         at = pl.ds(c * step, step)
         term = lax.dot_general(h_v[:, at], pi_v[:, at], nt, preferred_element_type=jnp.float32)
         total = term if total is None else total + term
     part[:, :width] = total
 
-    pl.semaphore_wait(barrier, (n_t - 1) + (n_dp - 1))
+    pl.semaphore_wait(barrier, (n_t - 1) + groups * (n_dp - 1))
 
     def a_copy(k):
         peer = lax.rem(me_t + k, n_t)
@@ -142,54 +151,80 @@
     for k, copy in enumerate(a_copies):
         copy.wait_recv()
         mine = mine + landed[k]
-    tokens[me_dp] = mine
-
-    def b_copy(k, slot):
+    my_slot = me_dp * n_t + me_t
+    tokens[my_slot] = mine
+
+    def slot_of(k, m):
+        return lax.rem(me_dp + k, n_dp) * n_t + lax.rem(me_t + m * pair, n_t)
+
+    def b_copy(k, m, slot):
         return pltpu.make_async_remote_copy(
             src_ref=tokens.at[slot],
             dst_ref=tokens.at[slot],
-            send_sem=b_send.at[k - 1],
-            recv_sem=b_recv.at[k - 1],
-            device_id={"dp": lax.rem(me_dp + k, n_dp)},
+            send_sem=b_send.at[k, m],
+            recv_sem=b_recv.at[k, m],
+            device_id={"dp": lax.rem(me_dp + k, n_dp), "tensor": lax.rem(me_t + m * pair, n_t)},
             device_id_type=MESH,
         )
 
-    repeat(1, n_dp, lambda k: b_copy(k, me_dp).start())
-    repeat(1, n_dp, lambda k: b_copy(k, lax.rem(me_dp + n_dp - k, n_dp)).wait_recv())
+    def c_copy(k, m, slot):
+        return pltpu.make_async_remote_copy(
+            src_ref=tokens.at[slot],
+            dst_ref=tokens.at[slot],
+            send_sem=c_send.at[k, m],
+            recv_sem=c_recv.at[k, m],
+            device_id={"tensor": other},
+            device_id_type=MESH,
+        )
+
+    def send(k):
+        for m in range(groups):
+            if not (isinstance(k, int) and k == 0 and m == 0):
+                b_copy(k, m, my_slot).start()
+
+    def take(k):
+        for m in range(groups):
+            slot = slot_of(n_dp - k, groups - m)
+            if not (isinstance(k, int) and k == 0 and m == 0):
+                b_copy(k, m, slot).wait_recv()
+            if pair == 2:
+                c_copy(k, m, slot).start()
+
+    def other_of(slot):
+        return slot + 1 - 2 * lax.rem(slot, 2)
+
+    def take_other(k):
+        for m in range(groups):
+            slot = slot_of(n_dp - k, groups - m)
+            c_copy(k, m, other_of(slot)).wait_recv()
+
+    def sent(k):
+        for m in range(groups):
+            if not (isinstance(k, int) and k == 0 and m == 0):
+                b_copy(k, m, my_slot).wait_send()
+            if pair == 2:
+                c_copy(k, m, slot_of(n_dp - k, groups - m)).wait_send()
+
+    send(0)
+    repeat(1, n_dp, send)
+    take(0)
+    repeat(1, n_dp, take)
+    if pair == 2:
+        take_other(0)
+        repeat(1, n_dp, take_other)
 
     upper = lax.broadcasted_iota(jnp.int32, (width, 2 * width), 1) >= width
-    upper_half = lax.broadcasted_iota(jnp.int32, (width // 2, 2 * width), 1) >= width
     upper1 = lax.broadcasted_iota(jnp.int32, (1, 2 * width), 1) >= width
     half = width // 2
-    covs = None
+    both = None
+    grams = []
     for s in range(seqs):
-        own = tokens[s * span : (s + 1) * span].reshape(span * share, 2 * width)
+        own = tokens[s * span * n_t : (s + 1) * span * n_t].reshape(span * rows, 2 * width)
         gram = lax.dot_general(own, own, tn, precision=HIGHEST, preferred_element_type=jnp.float32)
         cov = jnp.where(upper, gram[width:], gram[:width])
-        covs = cov if covs is None else covs + cov
-        swapped = pltpu.roll(gram[half:width], width, 1)
-        pay[me_t, pl.ds(width + s * half, half), :] = jnp.where(upper_half, gram[:half], swapped)
-    pay[me_t, :width, :] = covs
-
-    def c_copy(k, slot):
-        return pltpu.make_async_remote_copy(
-            src_ref=pay.at[slot],
-            dst_ref=pay.at[slot],
-            send_sem=c_send.at[k - 1],
-            recv_sem=c_recv.at[k - 1],
-            device_id={"tensor": lax.rem(me_t + k, n_t)},
-            device_id_type=MESH,
-        )
-
-    for k in range(1, n_t):
-        c_copy(k, me_t).start()
-    for k in range(1, n_t):
-        c_copy(k, lax.rem(me_t + n_t - k, n_t)).wait_recv()
-    full = pay[0]
-    for t in range(1, n_t):
-        full = full + pay[t]
-
-    both = full[:width] / token_count
+        both = cov if both is None else both + cov
+        grams.append(gram)
+    both = both / token_count
     row = lax.broadcasted_iota(jnp.int32, both.shape, 0)
     col = lax.broadcasted_iota(jnp.int32, both.shape, 1) % width
     diag = jnp.sum(jnp.where(row == col, both, 0.0), axis=0, keepdims=True)
@@ -203,8 +238,7 @@
 
     q_load.wait()
     for s in range(seqs):
-        packed = full[width + s * half : width + (s + 1) * half]
-        sketch = jnp.concatenate([pltpu.roll(packed, width, 1)[:, :width], packed[:, :width]], axis=0)
+        sketch = grams[s][:width, width:]
         left = jnp.dot(in_inv, sketch, precision=HIGHEST, preferred_element_type=jnp.float32)
         precond = jnp.dot(left, out_inv, precision=HIGHEST, preferred_element_type=jnp.float32)
         precond = (precond * factor).astype(jnp.bfloat16).astype(jnp.float32)
@@ -220,9 +254,8 @@
 
     for copy in a_copies:
         copy.wait_send()
-    repeat(1, n_dp, lambda k: b_copy(k, me_dp).wait_send())
-    for k in range(1, n_t):
-        c_copy(k, me_t).wait_send()
+    sent(0)
+    repeat(1, n_dp, sent)
 
 
 def solution(mesh):
@@ -235,12 +268,13 @@
         queries, flat = query_sketches.shape
         seqs = n_dp // min(32, n_dp)
         share = rows // n_t
+        groups = n_t // pair_of(n_t)
         dma = pltpu.SemaphoreType.DMA
         f32, bf16 = jnp.float32, jnp.bfloat16
         return pl.pallas_call(
             functools.partial(kernel, n_t, n_dp),
             out_shape=jax.ShapeDtypeStruct((seqs, queries), f32),
-            in_specs=[pl.BlockSpec(memory_space=pl.ANY)] * 5,
+            in_specs=[pl.BlockSpec(memory_space=pltpu.HBM)] * 5,
             out_specs=pl.BlockSpec(memory_space=pltpu.VMEM),
             scratch_shapes=[
                 pltpu.VMEM((rows, depth), bf16),
@@ -250,19 +284,18 @@
                 pltpu.VMEM((queries, flat), bf16),
                 pltpu.VMEM((rows, 2 * width), f32),
                 pltpu.VMEM((n_t - 1, share, 2 * width), f32),
-                pltpu.VMEM((n_dp, share, 2 * width), f32),
-                pltpu.VMEM((n_t, width + seqs * (width // 2), 2 * width), f32),
+                pltpu.VMEM((n_dp * n_t, share, 2 * width), f32),
                 dma((3,)),
                 dma((2 * IN_CHUNKS,)),
                 dma((n_t - 1,)),
                 dma((n_t - 1,)),
-                dma((n_dp - 1,)),
-                dma((n_dp - 1,)),
-                dma((n_t - 1,)),
-                dma((n_t - 1,)),
+                dma((n_dp, groups)),
+                dma((n_dp, groups)),
+                dma((n_dp, groups)),
+                dma((n_dp, groups)),
             ],
             compiler_params=pltpu.CompilerParams(
-                collective_id=0, has_side_effects=True, vmem_limit_bytes=48 * 1024 * 1024
+                collective_id=0, has_side_effects=True
             ),
         )(hidden_acts, out_grads, proj_in.T, proj_out.T, query_sketches)
 

time: 25.3 us -> 20 us (0.79); the launches traced: 24.9 us -> 19.9 us
  local copies, waits for them, and re-layouts: 6.08 us -> 1.19 us
    unnamed x11 -> x1, local copies, waits for them, and re-layouts: 6.08 us -> 1.19 us
where the time goes in v2:
time: 20 us; the launch traced here: 19.9 us
  Pallas kernels  18.7 us (94%)
  local copies, waits for them, and re-layouts  1.19 us (6%)
    pallas_call x1, Pallas kernels, shards(): pl.pallas_call(functools.partial(kernel, n_t, n_dp), out_shape=jax.ShapeD...  18.7 us
    unnamed x1, local copies, waits for them, and re-layouts  1.19 us

profile of v2, /device:TPU:1, one launch (start us, length us, event | category | flops | bytes accessed | tf_op | source)
XLA Modules:
  0.0 19.9 jit_solution(6023932552147009001)
XLA Ops:
  0.0 18.7 %shard_map.55 = f32[1,16]{1,0:T(1,128)} custom-call(bf16[128,7168]{1,0:T(8,128)(2,1)} %h_hbm.1, bf16[128,2048]{1,0:T(8,128)(2,1)} %g_hbm.1, bf16[64,7168]{1,0:T(8,128)(2,1)} %bitcast.2, bf16[64,2048]{1,0:T(8,128)(2,1)} %bitcast.3, bf16[16,4096]{1,0:T(8,128)(2,1)} %q_hbm.1), custom_call_target="tpu_custom_call" | custom-call | tf_op jit(solution)/shard_map/pallas_call | solution.py:274
  18.7 1.2 %copy.7 = f32[1,16]{1,0:T(1,128)} copy(f32[1,16]{1,0:T(1,128)} %shard_map.55) | data formatting | bytes 128

commit v3 on v2

--- a/solution.py
+++ b/solution.py
@@ -32,29 +32,24 @@
     lane = lax.broadcasted_iota(jnp.int32, shape, 1)
     col = lane % width
     side = lane - col
-    lane1 = lax.broadcasted_iota(jnp.int32, (1, shape[1]), 1)
-    col1 = lane1 % width
     m = both
     for k0 in range(0, width, BLOCK):
         js = range(BLOCK)
         cols = [jnp.take_along_axis(m, side + (k0 + j), axis=1) for j in js]
-        d = [[cols[j][k0 + i : k0 + i + 1, :] for j in js] for i in js]
-        in_block1 = (col1 >= k0) & (col1 < k0 + BLOCK)
-        w = [
-            jnp.where(in_block1, jnp.where(col1 == k0 + i, -1.0, 0.0), m[k0 + i : k0 + i + 1, :])
-            for i in js
-        ]
+        at = slice(k0, k0 + BLOCK)
+        d = [cols[j][at, :] for j in js]
+        unit = jnp.where(col[at] == row[at], -1.0, 0.0)
+        w = jnp.where((col[at] >= k0) & (col[at] < k0 + BLOCK), unit, m[at, :])
         for p in js:
-            r = 1.0 / d[p][p]
-            w[p] = w[p] * r
+            pivot_row = row[at] == k0 + p
+            f = d[p]
+            r = 1.0 / f[p : p + 1, :]
+            wp = w[p : p + 1, :] * r
+            w = jnp.where(pivot_row, wp, w - f * wp)
             for j in range(p + 1, BLOCK):
-                d[p][j] = d[p][j] * r
-            for i in js:
-                if i != p:
-                    f = d[i][p]
-                    w[i] = w[i] - f * w[p]
-                    for j in range(p + 1, BLOCK):
-                        d[i][j] = d[i][j] - f * d[p][j]
+                dp = d[j][p : p + 1, :] * r
+                d[j] = jnp.where(pivot_row, dp, d[j] - f * dp)
+        w = [w[j : j + 1, :] for j in js]
         in_rows = (row >= k0) & (row < k0 + BLOCK)
         in_cols = (col >= k0) & (col < k0 + BLOCK)
         m = jnp.where(in_rows | in_cols, 0.0, m)
@@ -72,15 +67,24 @@
     me_t = lax.axis_index("tensor")
     me_dp = lax.axis_index("dp")
     pair = pair_of(n_t)
-    groups = n_t // pair
-    other = me_t + 1 - 2 * lax.rem(me_t, 2)
     width = pi_v.shape[0]
     rows = part.shape[0]
-    share = rows // n_t
+    share = rows // pair
     span = min(32, n_dp)
     seqs = n_dp // span
     token_count = rows * n_dp
     factor = 1.0 / math.sqrt(rows * span)
+
+    barrier = pltpu.get_barrier_semaphore()
+
+    def greet_t(k):
+        pl.semaphore_signal(barrier, inc=1, device_id={"tensor": lax.rem(me_t + k, n_t)}, device_id_type=MESH)
+
+    def greet_dp(k):
+        pl.semaphore_signal(barrier, inc=1, device_id={"dp": lax.rem(me_dp + k, n_dp)}, device_id_type=MESH)
+
+    repeat(1, n_t, greet_t)
+    repeat(1, n_dp, greet_dp)
 
     step = h_v.shape[1] // IN_CHUNKS
     loads = [
@@ -104,19 +108,6 @@
             copy.start()
     q_load.start()
 
-    barrier = pltpu.get_barrier_semaphore()
-
-    def greet_t(k):
-        pl.semaphore_signal(barrier, inc=1, device_id={"tensor": lax.rem(me_t + k, n_t)}, device_id_type=MESH)
-
-    def greet_dp(k):
-        for m in range(groups):
-            peer = {"dp": lax.rem(me_dp + k, n_dp), "tensor": lax.rem(me_t + m * pair, n_t)}
-            pl.semaphore_signal(barrier, inc=1, device_id=peer, device_id_type=MESH)
-
-    repeat(1, n_t, greet_t)
-    repeat(1, n_dp, greet_dp)
-
     nt = (((1,), (1,)), ((), ()))
     tn = (((0,), (0,)), ((), ()))
     for copy in loads:
@@ -131,87 +122,67 @@
         total = term if total is None else total + term
     part[:, :width] = total
 
-    pl.semaphore_wait(barrier, (n_t - 1) + groups * (n_dp - 1))
-
-    def a_copy(k):
+    pl.semaphore_wait(barrier, (n_t - 1) + (n_dp - 1))
+
+    def share_of(t):
+        return pl.ds(pl.multiple_of(lax.rem(t, pair) * share, share), share)
+
+    def a_copy(k, slot):
         peer = lax.rem(me_t + k, n_t)
         return pltpu.make_async_remote_copy(
-            src_ref=part.at[pl.ds(pl.multiple_of(peer * share, share), share)],
-            dst_ref=landed.at[k - 1],
+            src_ref=part.at[share_of(peer)],
+            dst_ref=landed.at[slot],
             send_sem=a_send.at[k - 1],
             recv_sem=a_recv.at[k - 1],
             device_id={"tensor": peer},
             device_id_type=MESH,
         )
 
-    a_copies = [a_copy(k) for k in range(1, n_t)]
-    for copy in a_copies:
-        copy.start()
-    mine = part[pl.ds(pl.multiple_of(me_t * share, share), share), :]
-    for k, copy in enumerate(a_copies):
-        copy.wait_recv()
-        mine = mine + landed[k]
-    my_slot = me_dp * n_t + me_t
-    tokens[my_slot] = mine
-
-    def slot_of(k, m):
-        return lax.rem(me_dp + k, n_dp) * n_t + lax.rem(me_t + m * pair, n_t)
-
-    def b_copy(k, m, slot):
+    for k in range(1, n_t):
+        a_copy(k, me_t).start()
+    landed[me_t] = part[share_of(me_t), :]
+    for k in range(1, n_t):
+        a_copy(k, lax.rem(me_t + n_t - k, n_t)).wait_recv()
+    mine = landed[0]
+    for t in range(1, n_t):
+        mine = mine + landed[t]
+    side = lax.rem(me_t, pair)
+    tokens[me_dp * pair + side] = mine
+
+    def b_copy(k, dp):
+        slot = dp * pair + side
         return pltpu.make_async_remote_copy(
             src_ref=tokens.at[slot],
             dst_ref=tokens.at[slot],
-            send_sem=b_send.at[k, m],
-            recv_sem=b_recv.at[k, m],
-            device_id={"dp": lax.rem(me_dp + k, n_dp), "tensor": lax.rem(me_t + m * pair, n_t)},
+            send_sem=b_send.at[k],
+            recv_sem=b_recv.at[k],
+            device_id={"dp": lax.rem(me_dp + k, n_dp)},
             device_id_type=MESH,
         )
 
-    def c_copy(k, m, slot):
+    def c_copy(k, at_side):
+        slot = lax.rem(me_dp + n_dp - k, n_dp) * pair + at_side
         return pltpu.make_async_remote_copy(
             src_ref=tokens.at[slot],
             dst_ref=tokens.at[slot],
-            send_sem=c_send.at[k, m],
-            recv_sem=c_recv.at[k, m],
-            device_id={"tensor": other},
+            send_sem=c_send.at[k],
+            recv_sem=c_recv.at[k],
+            device_id={"tensor": me_t + 1 - 2 * side},
             device_id_type=MESH,
         )
 
-    def send(k):
-        for m in range(groups):
-            if not (isinstance(k, int) and k == 0 and m == 0):
-                b_copy(k, m, my_slot).start()
-
     def take(k):
-        for m in range(groups):
-            slot = slot_of(n_dp - k, groups - m)
-            if not (isinstance(k, int) and k == 0 and m == 0):
-                b_copy(k, m, slot).wait_recv()
-            if pair == 2:
-                c_copy(k, m, slot).start()
-
-    def other_of(slot):
-        return slot + 1 - 2 * lax.rem(slot, 2)
-
-    def take_other(k):
-        for m in range(groups):
-            slot = slot_of(n_dp - k, groups - m)
-            c_copy(k, m, other_of(slot)).wait_recv()
-
-    def sent(k):
-        for m in range(groups):
-            if not (isinstance(k, int) and k == 0 and m == 0):
-                b_copy(k, m, my_slot).wait_send()
-            if pair == 2:
-                c_copy(k, m, slot_of(n_dp - k, groups - m)).wait_send()
-
-    send(0)
-    repeat(1, n_dp, send)
-    take(0)
+        b_copy(k, lax.rem(me_dp + n_dp - k, n_dp)).wait_recv()
+        if pair == 2:
+            c_copy(k, side).start()
+
+    repeat(1, n_dp, lambda k: b_copy(k, me_dp).start())
+    if pair == 2:
+        c_copy(0, side).start()
     repeat(1, n_dp, take)
     if pair == 2:
-        take_other(0)
-        repeat(1, n_dp, take_other)
+        c_copy(0, 1 - side).wait_recv()
+        repeat(1, n_dp, lambda k: c_copy(k, 1 - side).wait_recv())
 
     upper = lax.broadcasted_iota(jnp.int32, (width, 2 * width), 1) >= width
     upper1 = lax.broadcasted_iota(jnp.int32, (1, 2 * width), 1) >= width
@@ -219,7 +190,7 @@
     both = None
     grams = []
     for s in range(seqs):
-        own = tokens[s * span * n_t : (s + 1) * span * n_t].reshape(span * rows, 2 * width)
+        own = tokens[s * span * pair : (s + 1) * span * pair].reshape(span * rows, 2 * width)
         gram = lax.dot_general(own, own, tn, precision=HIGHEST, preferred_element_type=jnp.float32)
         cov = jnp.where(upper, gram[width:], gram[:width])
         both = cov if both is None else both + cov
@@ -252,10 +223,12 @@
         scores = lax.dot_general(ones, acc, nt, precision=HIGHEST, preferred_element_type=jnp.float32)
         out_ref[s : s + 1, :] = scores[:1]
 
-    for copy in a_copies:
-        copy.wait_send()
-    sent(0)
-    repeat(1, n_dp, sent)
+    for k in range(1, n_t):
+        a_copy(k, me_t).wait_send()
+    repeat(1, n_dp, lambda k: b_copy(k, me_dp).wait_send())
+    if pair == 2:
+        c_copy(0, side).wait_send()
+        repeat(1, n_dp, lambda k: c_copy(k, side).wait_send())
 
 
 def solution(mesh):
@@ -267,8 +240,8 @@
         width = proj_in.shape[1]
         queries, flat = query_sketches.shape
         seqs = n_dp // min(32, n_dp)
-        share = rows // n_t
-        groups = n_t // pair_of(n_t)
+        pair = pair_of(n_t)
+        share = rows // pair
         dma = pltpu.SemaphoreType.DMA
         f32, bf16 = jnp.float32, jnp.bfloat16
         return pl.pallas_call(
@@ -283,16 +256,16 @@
                 pltpu.VMEM((width, model), bf16),
                 pltpu.VMEM((queries, flat), bf16),
                 pltpu.VMEM((rows, 2 * width), f32),
-                pltpu.VMEM((n_t - 1, share, 2 * width), f32),
-                pltpu.VMEM((n_dp * n_t, share, 2 * width), f32),
+                pltpu.VMEM((n_t, share, 2 * width), f32),
+                pltpu.VMEM((n_dp * pair, share, 2 * width), f32),
                 dma((3,)),
                 dma((2 * IN_CHUNKS,)),
                 dma((n_t - 1,)),
                 dma((n_t - 1,)),
-                dma((n_dp, groups)),
-                dma((n_dp, groups)),
-                dma((n_dp, groups)),
-                dma((n_dp, groups)),
+                dma((n_dp,)),
+                dma((n_dp,)),
+                dma((n_dp,)),
+                dma((n_dp,)),
             ],
             compiler_params=pltpu.CompilerParams(
                 collective_id=0, has_side_effects=True

time: 20 us -> 20 us (level)
  no operation moved by 1% of the time
where the time goes in v3:
time: 20 us; the launch traced here: 19.8 us
  Pallas kernels  18.6 us (93%)
  local copies, waits for them, and re-layouts  1.19 us (6%)
    pallas_call x1, Pallas kernels, shards(): pl.pallas_call(functools.partial(kernel, n_t, n_dp), out_shape=jax.ShapeD...  18.6 us
    unnamed x1, local copies, waits for them, and re-layouts  1.19 us

profile of v3, /device:TPU:1, one launch (start us, length us, event | category | flops | bytes accessed | tf_op | source)
XLA Modules:
  0.0 19.8 jit_solution(7327849209238756532)
XLA Ops:
  0.0 18.6 %shard_map.55 = f32[1,16]{1,0:T(1,128)} custom-call(bf16[128,7168]{1,0:T(8,128)(2,1)} %h_hbm.1, bf16[128,2048]{1,0:T(8,128)(2,1)} %g_hbm.1, bf16[64,7168]{1,0:T(8,128)(2,1)} %bitcast.2, bf16[64,2048]{1,0:T(8,128)(2,1)} %bitcast.3, bf16[16,4096]{1,0:T(8,128)(2,1)} %q_hbm.1), custom_call_target="tpu_custom_call" | custom-call | tf_op jit(solution)/shard_map/pallas_call | solution.py:247
  18.6 1.2 %copy.7 = f32[1,16]{1,0:T(1,128)} copy(f32[1,16]{1,0:T(1,128)} %shard_map.55) | data formatting | bytes 128
